TPU v7x, 32 devices: a whole 2x2x4 slice. The times are simulated.
32 devices in a mesh: pair: 8 (over z, x), orb: 4 (over y, core).
Axes of the slice: x: 2, y: 2, z: 4, core: 2. Of those that a mesh axis runs over, the one named last changes fastest.
Arguments:
- integrals: bfloat16 [512, 8, 128, 128], P('pair'), may hold values from -6 to 6
- screen: int32 [2, 512, 8], P(None, 'pair'), may hold values from 0 to 95
- occupied: bfloat16 [12288, 32], P(('pair', 'orb')), may hold values from -0.3125 to 0.3125
- virtual: bfloat16 [12288, 512], P(('pair', 'orb')), may hold values from -1.5 to 1.5
- pair_index: int32 [2, 512], replicated, may hold values from 0 to 12287
Outputs:
- mo_block: bfloat16 [4, 256, 512, 512], P('orb', 'pair')
All inputs are finite; a program needn't handle non-finite values.
Results may differ from a plain program's by a relative error of at most 0.0064.
Values may be sent and summed in bfloat16 or wider, within the bound.
A program may use at most 192 MiB of HBM per device.

v0:
```python
import jax
import jax.numpy as jnp
from jax import lax
from jax.sharding import PartitionSpec as P

BLK = 128


def body(integrals, screen, occupied, virtual, pair_index):
    occ_all, vir_all = (
        lax.all_gather(occupied, ("pair", "orb"), axis=0, tiled=True),
        lax.all_gather(virtual, ("pair", "orb"), axis=0, tiled=True),
    )
    orb_count = lax.axis_size("orb")
    first_count = occ_all.shape[1] // orb_count
    own_cols = lax.dynamic_slice_in_dim(
        occ_all, lax.axis_index("orb") * first_count, first_count, 1
    )
    block_count = occ_all.shape[0] // BLK
    blocks_all = occ_all.reshape(block_count, BLK, occ_all.shape[1])
    blocks_own = own_cols.reshape(block_count, BLK, first_count)
    coef_m = blocks_own[screen[0]]
    coef_n = blocks_all[screen[1]]
    half_one = jnp.einsum(
        "pkmn,pkmi->pkni", integrals, coef_m, preferred_element_type=jnp.float32
    ).astype(jnp.bfloat16)
    half = jnp.einsum(
        "pknj,pkni->pji", coef_n, half_one, preferred_element_type=jnp.float32
    ).astype(jnp.bfloat16)
    local_rows = half.reshape(half.shape[0], half.shape[1] * first_count)
    owned = lax.all_to_all(local_rows, "pair", split_axis=1, concat_axis=0, tiled=True)
    left = vir_all[pair_index[0]]
    right = vir_all[pair_index[1]]
    weighted = (
        left[:, None, :].astype(jnp.float32) * owned[:, :, None].astype(jnp.float32)
    ).astype(jnp.bfloat16)
    pair_total = weighted.shape[0]
    owned_count = weighted.shape[1]
    width = weighted.shape[2]
    flat = weighted.reshape(pair_total, owned_count * width)
    result = lax.dot_general(
        flat, right, (((0,), (0,)), ((), ())), preferred_element_type=jnp.float32
    )
    return result.astype(jnp.bfloat16).reshape(1, owned_count, width, width)


def solution(mesh):
    placed = (
        P("pair", None, None, None),
        P(None, "pair", None),
        P(("pair", "orb"), None),
        P(("pair", "orb"), None),
        P(),
    )
    return jax.shard_map(
        body, mesh=mesh, in_specs=placed, out_specs=P("orb", "pair", None, None), check_vma=False
    )
```

profile of v0, /device:TPU:0, one launch (start us, length us, event | category | flops | bytes accessed | tf_op | source)
XLA Modules:
  0.0 167.4 jit_solution(7457111887382019653)
XLA Ops:
  6.5 0.0 all-gather.2.cloned.1.call-start
  6.5 0.7 all-gather.2.cloned.1.call-update
  7.3 0.7 compare_select_fusion.2
  8.0 0.1 copy.12
  8.1 0.1 reshape.167
  8.1 0.1 copy.10
  8.2 0.1 reshape.159
  8.3 47.2 %all_gather.7 = bf16[12288,32]{0,1:T(8,128)(2,1)S(1)} all-gather(bf16[384,32]{0,1:T(8,128)(2,1)} %param.7), channel_id=1, replica_groups=mesh['pair'=8,'orb'=4] {'pair','orb'}, dimensions={0}, use_global_device_ids=true | all-gather | bytes 811008 | tf_op jit(solution)/shard_map/all_gather | solution.py:11
  55.5 1.8 %gather_fusion.2 = bf16[512,128,8]{1,2,0:T(8,128)(2,1)S(1)} fusion(bf16[96,128,8]{1,2,0:T(8,128)(2,1)S(1)} %dynamic-slice_bitcast_fusion, s32[1024]{0:T(1024)S(1)} %pad_clamp_fusion.1), kind=kCustom, calls=%fused_computation.2 | custom fusion | bytes 2099200 | tf_op jit(solution)/shard_map/gather | solution.py:22
  57.4 0.1 copy_bitcast_fusion
  57.5 3.5 %gather_fusion.1 = bf16[512,128,32]{1,2,0:T(8,128)(2,1)} fusion(bf16[96,128,32]{1,2,0:T(8,128)(2,1)S(1)} %copy_bitcast_fusion, s32[1024]{0:T(1024)S(1)} %pad_clamp_fusion.2), kind=kCustom, calls=%fused_computation.1 | custom fusion | bytes 8390656 | tf_op jit(solution)/shard_map/gather | solution.py:23
  61.0 0.0 copy-start
  61.0 9.9 %fusion.1 = bf16[64,32,8]{1,2,0:T(8,128)(2,1)S(1)} fusion(bf16[64,8,128,32]{2,3,1,0:T(8,128)(2,1)} %bitcast.51, bf16[64,8,128,8]{2,3,1,0:T(8,128)(2,1)S(1)} %bitcast.50, bf16[64,8,128,128]{3,2,1,0:T(8,128)(2,1)} %param.5), kind=kOutput, calls=%fused_computation.9 | convolution fusion | flops 168312832 | bytes 22052864 | tf_op jit(solution)/shard_map/pknj,pkni->pji/dot_general | solution.py:27
  70.9 0.1 copy.13
  71.1 0.7 reshape.184
  71.8 3.5 %all-to-all-start = ((bf16[8,2,1024]{2,1,0:T(2,128)(2,1)}), bf16[8,2,1024]{2,1,0:T(2,128)(2,1)S(1)}, u32[]{:S(2)}, u32[]{:S(2)}) async-start(bf16[8,2,1024]{2,1,0:T(2,128)(2,1)} %reshape.184), calls=%async_computation | async-start | bytes 65536 | tf_op jit(solution)/shard_map/all_to_all | solution.py:31
  75.3 0.0 copy-done
  75.4 6.9 %all-to-all-done = bf16[8,2,1024]{2,1,0:T(2,128)(2,1)S(1)} async-done(((bf16[8,2,1024]{2,1,0:T(2,128)(2,1)}), bf16[8,2,1024]{2,1,0:T(2,128)(2,1)S(1)}, u32[]{:S(2)}, u32[]{:S(2)}) %all-to-all-start) | async-done | bytes 32800 | tf_op jit(solution)/shard_map/all_to_all | solution.py:31
  82.2 0.1 reshape.185
  82.4 0.1 copy.17
  82.5 27.9 %all-gather.2.cloned.1.call-done = bf16[12288,512]{1,0:T(8,128)(2,1)} async-done(((bf16[384,512]{1,0:T(8,128)(2,1)}), bf16[12288,512]{1,0:T(8,128)(2,1)}) %all-gather.2.cloned.1.call-update) | async-done | bytes 12582928 | tf_op jit(solution)/shard_map/all_gather | solution.py:12
  110.5 8.2 %gather_fusion = bf16[512,512]{1,0:T(8,128)(2,1)S(1)} fusion(bf16[12288,512]{1,0:T(8,128)(2,1)} %all-gather.2.cloned.1.call-done, s32[1024]{0:T(1024)S(1)} %pad_clamp_fusion.3), kind=kCustom, calls=%fused_computation | custom fusion | bytes 1050624 | tf_op jit(solution)/shard_map/gather | solution.py:32
  118.6 0.1 convert_element_type.41
  118.8 3.1 %multiply_convert_fusion = bf16[512,32,512]{2,1,0:T(8,128)(2,1)S(1)} fusion(f32[512,32]{1,0:T(8,128)S(1)} %bitcast.54, f32[512,512]{1,0:T(8,128)S(1)} %convert_element_type.41), kind=kLoop, calls=%fused_computation.4 | loop fusion | flops 16777216 | bytes 17891328 | tf_op jit(solution)/shard_map/convert_element_type | solution.py:36
  121.8 12.2 %copy.20 = bf16[64,8,32,512]{3,1,2,0:T(8,128)(2,1)} copy(bf16[64,8,32,512]{3,2,1,0:T(8,128)(2,1)S(1)} %bitcast.52) | data formatting | bytes 33554432
  134.0 8.2 %gather_fusion.3 = bf16[512,512]{1,0:T(8,128)(2,1)S(1)} fusion(bf16[12288,512]{1,0:T(8,128)(2,1)} %all-gather.2.cloned.1.call-done, s32[1024]{0:T(1024)S(1)} %pad_clamp_fusion), kind=kCustom, calls=%fused_computation.3 | custom fusion | bytes 1050624 | tf_op jit(solution)/shard_map/gather | solution.py:33
  142.2 18.4 %convolution_convert_fusion = bf16[16384,512]{1,0:T(8,128)(2,1)} fusion(bf16[512,16384]{1,0:T(8,128)(2,1)} %bitcast.53, bf16[512,512]{1,0:T(8,128)(2,1)S(1)} %gather_fusion.3), kind=kOutput, calls=%fused_computation.5 | convolution fusion | flops 8598323200 | bytes 34078720 | tf_op jit(solution)/shard_map/dot_general | solution.py:41
  (8 shorter events, 0.1 us)
Async XLA Ops:
  6.5 103.9 %all-gather.2.cloned.1.call-start = ((), (), s32[]{:S(2)}) async-start(), calls=%async_computation.1 | async-start | bytes 12976128 | tf_op jit(solution)/shard_map/all_gather | solution.py:12
  61.0 14.3 %copy-start = (s32[2,512]{1,0:T(2,128)S(1)}, s32[2,512]{1,0:T(2,128)}, u32[]{:S(2)}) copy-start(s32[2,512]{1,0:T(2,128)} %param.9) | copy-start | bytes 12292
  71.8 10.4 %all-to-all-start = ((bf16[8,2,1024]{2,1,0:T(2,128)(2,1)}), bf16[8,2,1024]{2,1,0:T(2,128)(2,1)S(1)}, u32[]{:S(2)}, u32[]{:S(2)}) async-start(bf16[8,2,1024]{2,1,0:T(2,128)(2,1)} %reshape.184), calls=%async_computation | async-start | bytes 65536 | tf_op jit(solution)/shard_map/all_to_all | solution.py:31
Sparse Core Ops, SparseCore 0:
  10.2 100.1 all-gather.1
where the time goes:
time: 168 us; the launch traced here: 167 us
  blocking collectives  47.2 us (28%)
  waiting for transfers between devices  35.5 us (21%)
  local copies, waits for them, and re-layouts  35.5 us (21%)
  matrix products  28.3 us (17%)
  between operations  13.5 us (8%)
  other arithmetic  3.93 us (2%)
  starting transfers between devices  3.52 us (2%)
    all_gather x1, blocking collectives, body(): lax.all_gather(occupied, ('pair', 'orb'), axis=0, tiled=True)  47.2 us
    all_gather x1, waiting for transfers between devices, body(): lax.all_gather(virtual, ('pair', 'orb'), axis=0, tiled=True)  27.9 us
    dot_general x1, matrix products, body(): lax.dot_general(flat, right, (((0,), (0,)), ((), ())), preferred_element_...  18.4 us
    unnamed x6, local copies, waits for them, and re-layouts  13 us
    dot_general x1, matrix products, body(): jnp.einsum('pknj,pkni->pji', coef_n, half_one, preferred_element_type=jnp...  9.87 us
    gather x1, local copies, waits for them, and re-layouts, body(): right = vir_all[pair_index[1]]  8.18 us
    gather x1, local copies, waits for them, and re-layouts, body(): left = vir_all[pair_index[0]]  8.18 us
    all_to_all x1, waiting for transfers between devices, body(): lax.all_to_all(local_rows, 'pair', split_axis=1, concat_axis=0, tiled=True)  6.85 us
  transfers between devices with their start and end apart: 2, of which 2 were waited for; matrix products, arithmetic and copies ran while one was open for 10% of the time, Pallas kernels for 0%

commit v1 on v0

v1 whole, which is shorter than its diff:
```python
import functools

import jax
import jax.numpy as jnp
from jax import lax
from jax.experimental import pallas as pl
from jax.experimental.pallas import tpu as pltpu
from jax.sharding import PartitionSpec as P

BLK = 128
MESH = pl.DeviceIdType.MESH
BF = jnp.bfloat16
F32 = jnp.float32


def exchange_kernel(
    shape,
    screen_ref,
    ints_ref,
    occ_ref,
    vir_ref,
    pidx_ref,
    tab_ref,
    half_ref,
    ints,
    panel,
    by_core,
    by_x,
    from_y,
    mine_y,
    from_z,
    halves,
    outgoing,
    int_sem,
    ssem,
    rsem,
    a2a_s,
    a2a_r,
):
    n_pair, n_orb, nz, own_pairs, slots = shape
    n_dev = n_pair * n_orb
    d = lax.axis_index("pair")
    o = lax.axis_index("orb")
    z, x = d // 2, d % 2
    y, c = o // 2, o % 2
    me = d * n_orb + o
    rows = vir_ref.shape[0]
    width = vir_ref.shape[1]
    quarter = width // 4
    pairs = tab_ref.shape[2]
    count = own_pairs * slots
    i_count = occ_ref.shape[0]

    fetch = pltpu.make_async_copy(ints_ref.at[pl.ds(o * count, count)], ints, int_sem)
    fetch.start()

    per_dev = rows // BLK
    blocks = per_dev * nz

    def occ_at(xx, yy, cc):
        return ((xx * 2 + yy) * 2 + cc) * blocks

    for k in range(per_dev):
        panel[occ_at(x, y, c) + z * per_dev + k] = occ_ref[:, k * BLK : (k + 1) * BLK]

    barrier = pltpu.get_barrier_semaphore()

    def greet(k, carry):
        t = lax.rem(me + k, n_dev)
        pl.semaphore_signal(
            barrier, inc=1, device_id=(t // n_orb, t % n_orb), device_id_type=MESH
        )
        return carry

    lax.fori_loop(1, n_dev, greet, 0)
    pl.semaphore_wait(barrier, n_dev - 1)

    x_peer = (z * 2 + 1 - x, o)
    y_peer = (d, (1 - y) * 2 + c)
    c_peer = (d, y * 2 + 1 - c)
    used = [0]

    def send(src, dst, peer):
        n = used[0]
        used[0] += 1
        copy = pltpu.make_async_remote_copy(
            src_ref=src,
            dst_ref=dst,
            send_sem=ssem.at[n],
            recv_sem=rsem.at[n],
            device_id=peer,
            device_id_type=MESH,
        )
        copy.start()
        return copy

    started = []

    def z_spread(ref):
        out = []
        for k in range(1, nz):
            zz = lax.rem(z + k, nz)
            out.append(send(ref, ref, (zz * 2 + x, o)))
        return out

    occ_own = panel.at[pl.ds(occ_at(x, y, c) + z * per_dev, per_dev)]
    occ_z = z_spread(occ_own)
    half_w = 2 * quarter
    away = pl.multiple_of((1 - c) * half_w, half_w)
    home = pl.multiple_of(c * half_w, half_w)
    vir_c = send(vir_ref.at[:, pl.ds(away, half_w)], by_core.at[c], c_peer)
    by_core[c] = vir_ref[:, pl.ds(home, half_w)]
    vir_c.wait()
    away_x = pl.multiple_of((1 - x) * quarter, quarter)
    home_x = pl.multiple_of(x * quarter, quarter)
    vir_x = send(by_core.at[:, :, pl.ds(away_x, quarter)], by_x.at[x], x_peer)
    by_x[x] = by_core[:, :, pl.ds(home_x, quarter)]
    for copy in occ_z:
        copy.wait()

    def plane_first(view):
        own = view(x, y, c, None)
        return [send(own, own, peer) for peer in (x_peer, y_peer, c_peer)]

    def plane_second(view, first):
        first[0].wait()
        from_x = view(1 - x, y, c, None)
        part = view(1 - x, y, c, 0)
        out = [send(part, part, y_peer), send(from_x, from_x, c_peer)]
        first[1].wait()
        from_yy = view(x, 1 - y, c, None)
        part = view(x, 1 - y, c, 1)
        return out + [send(part, part, x_peer), send(from_yy, from_yy, c_peer)]

    def plane_third(view, first, second):
        second[0].wait()
        second[2].wait()
        diag = view(1 - x, 1 - y, c, None)
        third = send(diag, diag, c_peer)
        first[2].wait()
        second[1].wait()
        second[3].wait()
        return third

    def occ_view(xx, yy, cc, part):
        if part is None:
            return panel.at[pl.ds(occ_at(xx, yy, cc), blocks)]
        h = blocks // 2
        return panel.at[pl.ds(occ_at(xx, yy, cc) + part * h, h)]

    occ_1 = plane_first(occ_view)
    occ_2 = plane_second(occ_view, occ_1)

    vir_x.wait()

    def picked(which):
        total = jnp.zeros((pairs, quarter), F32)
        want = pidx_ref[which]
        for xx in range(2):
            for cc in range(2):
                base = ((z * 2 + xx) * n_orb + y * 2 + cc) * rows
                at = lax.broadcasted_iota(jnp.int32, (pairs, rows), 1) + base
                hot = jnp.where(at == want, 1.0, 0.0).astype(BF)
                total += jnp.dot(hot, by_x[xx, cc], preferred_element_type=F32)
        return total.astype(BF)

    mine_y[0] = picked(1 - y)
    vir_y = send(mine_y.at[0], from_y, y_peer)
    mine_y[1] = picked(y)
    vir_y.wait()
    mine_y[1] = mine_y[1] + from_y[...]
    share = pairs // nz
    vir_z = []
    for k in range(1, nz):
        zz = lax.rem(z + k, nz)
        vir_z.append(
            send(
                mine_y.at[1, pl.ds(pl.multiple_of(zz * share, share), share)],
                from_z.at[k - 1],
                (zz * 2 + x, o),
            )
        )
    occ_3 = plane_third(occ_view, occ_1, occ_2)
    for copy in vir_z:
        copy.wait()
    at_z = pl.ds(pl.multiple_of(z * share, share), share)
    total = mine_y[1, at_z]
    for k in range(nz - 1):
        total = total + from_z[k]
    tab_ref[c * 2 + x, y, at_z] = total
    tab_z = z_spread(tab_ref.at[c * 2 + x, y, at_z])

    fetch.wait()
    occ_3.wait()

    def transform(p, carry):
        firsts, seconds = [], []
        for s in range(slots):
            block_m = panel[screen_ref[0, p * slots + s]]
            first = jnp.dot(block_m, ints[p * slots + s], preferred_element_type=F32)
            firsts.append(first.astype(BF))
            seconds.append(panel[screen_ref[1, p * slots + s]])
        halves[p] = lax.dot_general(
            jnp.concatenate(seconds, axis=1),
            jnp.concatenate(firsts, axis=1),
            (((1,), (1,)), ((), ())),
            preferred_element_type=F32,
        )
        return carry

    quarter_pairs = own_pairs // 4
    lax.fori_loop(0, quarter_pairs, transform, 0)

    for copy in tab_z:
        copy.wait()

    def tab_view(xx, yy, cc, part):
        if part is None:
            return tab_ref.at[cc * 2 + xx, yy]
        h = pairs // 2
        return tab_ref.at[cc * 2 + xx, yy, pl.ds(part * h, h)]

    tab_1 = plane_first(tab_view)
    lax.fori_loop(quarter_pairs, own_pairs, transform, 0)

    flat = jnp.concatenate([halves[p] for p in range(own_pairs)], axis=1).astype(BF)
    size = own_pairs * i_count
    row = lax.broadcasted_iota(jnp.int32, (size, size), 0)
    col = lax.broadcasted_iota(jnp.int32, (size, size), 1)
    source = (col % own_pairs) * i_count + col // own_pairs
    swap = jnp.where(row == source, 1.0, 0.0).astype(BF)
    swapped = jnp.dot(flat, swap, preferred_element_type=F32)
    j_own = i_count // n_pair
    lanes = size // n_orb
    for dd in range(n_pair):
        for oo in range(n_orb):
            outgoing[dd * n_orb + oo] = swapped[
                dd * j_own : (dd + 1) * j_own, oo * lanes : (oo + 1) * lanes
            ]
    half_ref[me] = outgoing[me]

    def a2a(k):
        t = lax.rem(me + k, n_dev)
        return pltpu.make_async_remote_copy(
            src_ref=outgoing.at[t],
            dst_ref=half_ref.at[me],
            send_sem=a2a_s.at[k],
            recv_sem=a2a_r.at[k],
            device_id=(t // n_orb, t % n_orb),
            device_id_type=MESH,
        )

    def a2a_start(k, carry):
        a2a(k).start()
        return carry

    def a2a_wait(k, carry):
        a2a(k).wait()
        return carry

    lax.fori_loop(1, n_dev, a2a_start, 0)
    tab_2 = plane_second(tab_view, tab_1)
    tab_3 = plane_third(tab_view, tab_1, tab_2)
    lax.fori_loop(1, n_dev, a2a_wait, 0)
    tab_3.wait()


def expand_kernel(per_step, half_ref, tab_ref, out_ref, left_t, right):
    step = pl.program_id(0)
    width = left_t.shape[0]
    quarter = width // 4

    @pl.when(step == 0)
    def _():
        for q in range(4):
            left_t[q * quarter : (q + 1) * quarter, :] = tab_ref[q, 0].T
            right[:, q * quarter : (q + 1) * quarter] = tab_ref[q, 1]

    for k in range(per_step):
        weighted = left_t[...] * half_ref[step * per_step + k]
        out_ref[0, k] = jnp.dot(
            weighted, right[...], preferred_element_type=F32
        ).astype(BF)


def fast_body(integrals, screen, occupied, virtual, pair_index):
    n_pair, n_orb = lax.axis_size("pair"), lax.axis_size("orb")
    n_dev = n_pair * n_orb
    nz = n_pair // 2
    rows, width = virtual.shape
    pairs = pair_index.shape[1]
    i_count = occupied.shape[1]
    slots = integrals.shape[1]
    own_pairs = integrals.shape[0] // n_orb
    per_dev = rows // BLK
    own_screen = lax.dynamic_slice_in_dim(
        screen, lax.axis_index("orb") * own_pairs, own_pairs, 1
    ).reshape(2, own_pairs * slots)
    dev, k = own_screen // per_dev, own_screen % per_dev
    dz, rest = dev // (2 * n_orb), dev % (2 * n_orb)
    own_screen = (rest * nz + dz) * per_dev + k
    share = pairs // nz
    j_own = i_count // n_pair
    lanes = own_pairs * i_count // n_orb
    sends = 2 * (nz - 1) + 8 + 3 + (nz - 1) + 8
    vmem = pl.BlockSpec(memory_space=pltpu.VMEM)
    table, half = pl.pallas_call(
        functools.partial(exchange_kernel, (n_pair, n_orb, nz, own_pairs, slots)),
        out_shape=(
            jax.ShapeDtypeStruct((4, 2, pairs, width // 4), BF),
            jax.ShapeDtypeStruct((n_dev, j_own, lanes), F32),
        ),
        in_specs=[
            pl.BlockSpec(memory_space=pltpu.SMEM),
            pl.BlockSpec(memory_space=pl.ANY),
            vmem,
            vmem,
            vmem,
        ],
        out_specs=(vmem, vmem),
        scratch_shapes=[
            pltpu.VMEM((own_pairs * slots, BLK, BLK), BF),
            pltpu.VMEM((n_dev * per_dev, i_count, BLK), BF),
            pltpu.VMEM((2, rows, width // 2), BF),
            pltpu.VMEM((2, 2, rows, width // 4), BF),
            pltpu.VMEM((pairs, width // 4), BF),
            pltpu.VMEM((2, pairs, width // 4), BF),
            pltpu.VMEM((nz - 1, share, width // 4), BF),
            pltpu.VMEM((own_pairs, i_count, i_count), F32),
            pltpu.VMEM((n_dev, j_own, lanes), F32),
            pltpu.SemaphoreType.DMA,
            pltpu.SemaphoreType.DMA((sends,)),
            pltpu.SemaphoreType.DMA((sends,)),
            pltpu.SemaphoreType.DMA((n_dev,)),
            pltpu.SemaphoreType.DMA((n_dev,)),
        ],
        compiler_params=pltpu.CompilerParams(
            collective_id=0, has_side_effects=True, vmem_limit_bytes=48 * 2**20
        ),
    )(
        own_screen,
        integrals.reshape(-1, BLK, BLK),
        occupied.T,
        virtual,
        pair_index[:, :, None],
    )
    k_own = i_count // n_orb
    half = half.reshape(n_dev, j_own, k_own, own_pairs).transpose(1, 2, 0, 3)
    half = half.reshape(j_own * k_own, 1, pairs).astype(BF)
    count = j_own * k_own
    per_step = 2
    return pl.pallas_call(
        functools.partial(expand_kernel, per_step),
        grid=(count // per_step,),
        out_shape=jax.ShapeDtypeStruct((1, count, width, width), BF),
        in_specs=[vmem, vmem],
        out_specs=pl.BlockSpec((1, per_step, width, width), lambda s: (0, s, 0, 0)),
        scratch_shapes=[pltpu.VMEM((width, pairs), BF), pltpu.VMEM((pairs, width), BF)],
        compiler_params=pltpu.CompilerParams(vmem_limit_bytes=48 * 2**20),
    )(half, table)


def plain_body(integrals, screen, occupied, virtual, pair_index):
    occ_all = lax.all_gather(occupied, ("pair", "orb"), axis=0, tiled=True)
    vir_all = lax.all_gather(virtual, ("pair", "orb"), axis=0, tiled=True)
    first_count = occ_all.shape[1] // lax.axis_size("orb")
    own_cols = lax.dynamic_slice_in_dim(
        occ_all, lax.axis_index("orb") * first_count, first_count, 1
    )
    block_count = occ_all.shape[0] // BLK

    def blocks_of(cols, index):
        hot = jax.nn.one_hot(index.reshape(-1), block_count, dtype=BF)
        taken = jnp.dot(
            hot, cols.reshape(block_count, -1), preferred_element_type=F32
        ).astype(BF)
        return taken.reshape(index.shape + (BLK, cols.shape[1]))

    coef_m = blocks_of(own_cols, screen[0])
    coef_n = blocks_of(occ_all, screen[1])
    half_one = jnp.einsum(
        "pkmn,pkmi->pkni", integrals, coef_m, preferred_element_type=F32
    ).astype(BF)
    half = jnp.einsum(
        "pknj,pkni->pji", coef_n, half_one, preferred_element_type=F32
    ).astype(BF)
    local_rows = half.reshape(half.shape[0], -1)
    owned = lax.all_to_all(local_rows, "pair", split_axis=1, concat_axis=0, tiled=True)
    left = vir_all[pair_index[0]]
    right = vir_all[pair_index[1]]
    weighted = (left[:, None, :].astype(F32) * owned[:, :, None].astype(F32)).astype(BF)
    width = weighted.shape[2]
    flat = weighted.reshape(weighted.shape[0], -1)
    result = lax.dot_general(
        flat, right, (((0,), (0,)), ((), ())), preferred_element_type=F32
    )
    return result.astype(BF).reshape(1, -1, width, width)


def body(*args):
    n_pair, n_orb = lax.axis_size("pair"), lax.axis_size("orb")
    fits = (
        n_orb == 4
        and n_pair % 2 == 0
        and n_pair <= 8
        and args[2].shape[0] % BLK == 0
        and args[4].shape[1] == n_pair * args[0].shape[0]
    )
    return fast_body(*args) if fits else plain_body(*args)


def solution(mesh):
    placed = (
        P("pair", None, None, None),
        P(None, "pair", None),
        P(("pair", "orb"), None),
        P(("pair", "orb"), None),
        P(),
    )
    return jax.shard_map(
        body, mesh=mesh, in_specs=placed, out_specs=P("orb", "pair", None, None), check_vma=False
    )
```

time: 168 us -> 61.4 us (0.37)
  Pallas kernels: 0 us -> 55.8 us
  blocking collectives: 47.2 us -> 0 us
  waiting for transfers between devices: 35.5 us -> 0 us
  local copies, waits for them, and re-layouts: 35.5 us -> 3.65 us
  matrix products: 28.3 us -> 0 us
  between operations: 13.5 us -> 0.06 us
  starting transfers between devices: 3.52 us -> 0 us
  other arithmetic: 3.93 us -> 1.59 us
    pallas_call x0 -> x2, Pallas kernels: none -> 55.8 us  [the longest x1 41.4 us: fast_body(): pl.pallas_call(functools.partial(exchange_kernel, (n_pair, n_orb, nz, own...]
    all_gather x1 -> x0, blocking collectives: 47.2 us -> none  [body(): lax.all_gather(occupied, ('pair', 'orb'), axis=0, tiled=True)]
    dot_general x2 -> x0, matrix products: 28.3 us -> none  [the longest x1 18.4 us: body(): lax.dot_general(flat, right, (((0,), (0,)), ((), ())), preferred_element_...]
    all_gather x1 -> x0, waiting for transfers between devices: 27.9 us -> none  [body(): lax.all_gather(virtual, ('pair', 'orb'), axis=0, tiled=True)]
    gather x4 -> x0, local copies, waits for them, and re-layouts: 21.7 us -> none  [the longest x1 8.18 us: body(): right = vir_all[pair_index[1]]]
    unnamed x6 -> x4, local copies, waits for them, and re-layouts: 13 us -> 1.73 us
    all_to_all x1 -> x0, waiting for transfers between devices: 6.85 us -> none  [body(): lax.all_to_all(local_rows, 'pair', split_axis=1, concat_axis=0, tiled=True)]
    all_to_all x1 -> x0, starting transfers between devices: 3.52 us -> none  [body(): lax.all_to_all(local_rows, 'pair', split_axis=1, concat_axis=0, tiled=True)]
  transfers between devices with their start and end apart: 2 -> 0, of which waited for: 2 -> 0; matrix products, arithmetic and copies ran while one was open for 10% -> 0% of each run, Pallas kernels for 0% -> 0%
where the time goes in v1:
time: 61.4 us; the launch traced here: 61.1 us
  Pallas kernels  55.8 us (91%)
  local copies, waits for them, and re-layouts  3.65 us (6%)
  other arithmetic  1.59 us (3%)
    pallas_call x1, Pallas kernels, fast_body(): pl.pallas_call(functools.partial(exchange_kernel, (n_pair, n_orb, nz, own...  41.4 us
    pallas_call x1, Pallas kernels, fast_body(): pl.pallas_call(functools.partial(expand_kernel, per_step), grid=(count //...  14.4 us
    unnamed x4, local copies, waits for them, and re-layouts  1.73 us

profile of v1, /device:TPU:0, one launch (start us, length us, event | category | flops | bytes accessed | tf_op | source)
XLA Modules:
  0.0 61.1 jit_solution(14682939710282871537)
XLA Ops:
  0.0 0.8 %sign_compare_fusion = pred[2,16,8]{1,2,0:T(8,128)(4,1)S(1)} fusion(s32[2,64,8]{1,2,0:T(8,128)} %param.6, s32[]{:T(128)S(6)} %select_n.22), kind=kLoop, calls=%fused_computation | loop fusion | flops 512 | bytes 1284 | tf_op jit(solution)/shard_map/jit(floor_divide)/ne | solution.py:299
  0.8 0.1 copy.10
  0.9 0.1 ne.40
  1.0 0.8 %dynamic-slice_divide_fusion = (s32[2,16,8]{1,2,0:T(8,128)S(1)}, s32[2,16,8]{1,2,0:T(8,128)S(1)}) fusion(s32[2,64,8]{1,2,0:T(8,128)} %param.6, s32[]{:T(128)S(6)} %select_n.22), kind=kLoop, calls=%fused_computation.1 | loop fusion | flops 512 | bytes 3076 | tf_op jit(solution)/shard_map/jit(floor_divide)/div | solution.py:299
  1.8 0.1 copy.12
  1.8 0.1 div.18
  1.9 0.1 copy.11
  2.0 0.1 rem.39
  2.1 0.9 %copy.13.pidx_ref = s32[2,512,1]{2,1,0:T(8,128)S(1)} copy(s32[2,512,1]{1,0,2:T(2,128)} %bitcast.11) | data formatting | bytes 8192 | tf_op jit(solution)/shard_map/broadcast_in_dim | solution.py:345
  3.0 0.0 copy-start
  3.0 1.0 %copy-done = bf16[384,512]{1,0:T(8,128)(2,1)S(1)} copy-done((bf16[384,512]{1,0:T(8,128)(2,1)S(1)}, bf16[384,512]{1,0:T(8,128)(2,1)}, u32[]{:S(2)}) %copy-start) | copy-done | bytes 393240
  4.0 0.0 copy-start.1
  4.0 0.7 %copy-done.1 = bf16[384,32]{0,1:T(8,128)(2,1)S(1)} copy-done((bf16[384,32]{0,1:T(8,128)(2,1)S(1)}, bf16[384,32]{0,1:T(8,128)(2,1)}, u32[]{:S(2)}) %copy-start.1) | copy-done | bytes 24600
  4.8 41.4 %shard_map.55 = (bf16[4,2,512,128]{3,2,1,0:T(8,128)(2,1)S(1)}, f32[32,4,128]{2,1,0:T(4,128)S(1)}) custom-call(s32[2,128]{1,0:T(2,128)S(1)} %fusion.2.screen_ref, bf16[512,128,128]{2,1,0:T(8,128)(2,1)} %bitcast.9, bf16[32,384]{1,0:T(8,128)(2,1)S(1)} %bitcast.8, bf16[384,512]{1,0:T(8,128)(2,1)S(1)} %copy-done, s32[2,512,1]{2,1,0:T(8,128)S(1)} %copy.13.pidx_ref), custom_call_target="tpu_custom_call" | custom-call | tf_op jit(solution)/shard_map/pallas_call | solution.py:307
  46.2 0.1 copy.14
  46.4 0.2 copy.15
  46.6 0.2 convert_element_type.13.half_ref
  46.7 14.4 %shard_map.56 = bf16[1,32,512,512]{3,2,1,0:T(8,128)(2,1)} custom-call(bf16[32,1,512]{2,1,0:T(2,128)(2,1)S(1)} %convert_element_type.13.half_ref, bf16[4,2,512,128]{3,2,1,0:T(8,128)(2,1)S(1)} %get-tuple-element.8.tab_ref), custom_call_target="tpu_custom_call" | custom-call | tf_op jit(solution)/shard_map/pallas_call | solution.py:352
  (2 shorter events, 0.0 us)
Async XLA Ops:
  3.0 1.0 %copy-start = (bf16[384,512]{1,0:T(8,128)(2,1)S(1)}, bf16[384,512]{1,0:T(8,128)(2,1)}, u32[]{:S(2)}) copy-start(bf16[384,512]{1,0:T(8,128)(2,1)} %vir_ref.1) | copy-start | bytes 1179652
  4.0 0.7 %copy-start.1 = (bf16[384,32]{0,1:T(8,128)(2,1)S(1)}, bf16[384,32]{0,1:T(8,128)(2,1)}, u32[]{:S(2)}) copy-start(bf16[384,32]{0,1:T(8,128)(2,1)} %param.7) | copy-start | bytes 73732

commit v2 on v1

--- a/solution.py
+++ b/solution.py
@@ -24,14 +24,14 @@
     half_ref,
     ints,
     panel,
-    by_core,
-    by_x,
-    from_y,
-    mine_y,
+    got,
+    from_c,
+    mine,
     from_z,
     halves,
     outgoing,
     int_sem,
+    own_sem,
     ssem,
     rsem,
     a2a_s,
@@ -45,14 +45,21 @@
     y, c = o // 2, o % 2
     me = d * n_orb + o
     rows = vir_ref.shape[0]
-    width = vir_ref.shape[1]
-    quarter = width // 4
     pairs = tab_ref.shape[2]
     count = own_pairs * slots
     i_count = occ_ref.shape[0]
 
     fetch = pltpu.make_async_copy(ints_ref.at[pl.ds(o * count, count)], ints, int_sem)
     fetch.start()
+    quarter = vir_ref.shape[1] // 4
+
+    def columns(xx, yy):
+        return pl.ds(pl.multiple_of((xx * 2 + yy) * quarter, quarter), quarter)
+
+    vir_own = pltpu.make_async_copy(
+        vir_ref.at[:, columns(x, y)], got.at[x * 2 + y], own_sem.at[0]
+    )
+    vir_own.start()
 
     per_dev = rows // BLK
     blocks = per_dev * nz
@@ -60,8 +67,16 @@
     def occ_at(xx, yy, cc):
         return ((xx * 2 + yy) * 2 + cc) * blocks
 
-    for k in range(per_dev):
-        panel[occ_at(x, y, c) + z * per_dev + k] = occ_ref[:, k * BLK : (k + 1) * BLK]
+    occ_own = [
+        pltpu.make_async_copy(
+            occ_ref.at[:, k * BLK : (k + 1) * BLK],
+            panel.at[occ_at(x, y, c) + z * per_dev + k],
+            own_sem.at[1 + k],
+        )
+        for k in range(per_dev)
+    ]
+    for copy in occ_own:
+        copy.start()
 
     barrier = pltpu.get_barrier_semaphore()
 
@@ -78,6 +93,7 @@
     x_peer = (z * 2 + 1 - x, o)
     y_peer = (d, (1 - y) * 2 + c)
     c_peer = (d, y * 2 + 1 - c)
+    far_peer = (z * 2 + 1 - x, (1 - y) * 2 + c)
     used = [0]
 
     def send(src, dst, peer):
@@ -94,7 +110,6 @@
         copy.start()
         return copy
 
-    started = []
 
     def z_spread(ref):
         out = []
@@ -103,18 +118,18 @@
             out.append(send(ref, ref, (zz * 2 + x, o)))
         return out
 
+    vir_plane = [
+        send(vir_ref.at[:, columns(xx, yy)], got.at[x * 2 + y], peer)
+        for xx, yy, peer in (
+            (1 - x, y, x_peer),
+            (x, 1 - y, y_peer),
+            (1 - x, 1 - y, far_peer),
+        )
+    ]
+    for copy in occ_own:
+        copy.wait()
     occ_own = panel.at[pl.ds(occ_at(x, y, c) + z * per_dev, per_dev)]
     occ_z = z_spread(occ_own)
-    half_w = 2 * quarter
-    away = pl.multiple_of((1 - c) * half_w, half_w)
-    home = pl.multiple_of(c * half_w, half_w)
-    vir_c = send(vir_ref.at[:, pl.ds(away, half_w)], by_core.at[c], c_peer)
-    by_core[c] = vir_ref[:, pl.ds(home, half_w)]
-    vir_c.wait()
-    away_x = pl.multiple_of((1 - x) * quarter, quarter)
-    home_x = pl.multiple_of(x * quarter, quarter)
-    vir_x = send(by_core.at[:, :, pl.ds(away_x, quarter)], by_x.at[x], x_peer)
-    by_x[x] = by_core[:, :, pl.ds(home_x, quarter)]
     for copy in occ_z:
         copy.wait()
 
@@ -149,33 +164,34 @@
         return panel.at[pl.ds(occ_at(xx, yy, cc) + part * h, h)]
 
     occ_1 = plane_first(occ_view)
-    occ_2 = plane_second(occ_view, occ_1)
-
-    vir_x.wait()
+    vir_own.wait()
+    for copy in vir_plane:
+        copy.wait()
 
     def picked(which):
         total = jnp.zeros((pairs, quarter), F32)
-        want = pidx_ref[which]
+        want = jnp.broadcast_to(pidx_ref[pl.ds(which, 1)], (8, pairs)).T[:, :1]
         for xx in range(2):
-            for cc in range(2):
-                base = ((z * 2 + xx) * n_orb + y * 2 + cc) * rows
+            for yy in range(2):
+                base = ((z * 2 + xx) * n_orb + yy * 2 + c) * rows
                 at = lax.broadcasted_iota(jnp.int32, (pairs, rows), 1) + base
                 hot = jnp.where(at == want, 1.0, 0.0).astype(BF)
-                total += jnp.dot(hot, by_x[xx, cc], preferred_element_type=F32)
+                total += jnp.dot(hot, got[xx * 2 + yy], preferred_element_type=F32)
         return total.astype(BF)
 
-    mine_y[0] = picked(1 - y)
-    vir_y = send(mine_y.at[0], from_y, y_peer)
-    mine_y[1] = picked(y)
-    vir_y.wait()
-    mine_y[1] = mine_y[1] + from_y[...]
+    mine[0] = picked(1 - c)
+    vir_c = send(mine.at[0], from_c, c_peer)
+    mine[1] = picked(c)
+    occ_2 = plane_second(occ_view, occ_1)
+    vir_c.wait()
+    mine[1] = mine[1] + from_c[...]
     share = pairs // nz
     vir_z = []
     for k in range(1, nz):
         zz = lax.rem(z + k, nz)
         vir_z.append(
             send(
-                mine_y.at[1, pl.ds(pl.multiple_of(zz * share, share), share)],
+                mine.at[1, pl.ds(pl.multiple_of(zz * share, share), share)],
                 from_z.at[k - 1],
                 (zz * 2 + x, o),
             )
@@ -183,23 +199,43 @@
     occ_3 = plane_third(occ_view, occ_1, occ_2)
     for copy in vir_z:
         copy.wait()
-    at_z = pl.ds(pl.multiple_of(z * share, share), share)
-    total = mine_y[1, at_z]
+    def rows_of(k):
+        zz = lax.rem(z - k + nz, nz)
+        return pl.ds(pl.multiple_of(zz * share, share), share)
+
+    def tab_at(xx, yy, cc, k=None):
+        if k is None:
+            return tab_ref.at[xx * 2 + yy, cc]
+        return tab_ref.at[xx * 2 + yy, cc, rows_of(k)]
+
+    total = mine[1, rows_of(0)]
     for k in range(nz - 1):
         total = total + from_z[k]
-    tab_ref[c * 2 + x, y, at_z] = total
-    tab_z = z_spread(tab_ref.at[c * 2 + x, y, at_z])
+    tab_ref[x * 2 + y, c, rows_of(0)] = total
+    tab_z = z_spread(tab_at(x, y, c, 0))
+    tab_plane = []
+
+    def pass_on(k):
+        part = tab_at(x, y, c, k)
+        tab_plane.append([send(part, part, p) for p in (x_peer, y_peer, c_peer)])
+
+    pass_on(0)
 
     fetch.wait()
     occ_3.wait()
+
+    def place(block):
+        dev, k = lax.div(block, per_dev), lax.rem(block, per_dev)
+        dz, rest = lax.div(dev, 2 * n_orb), lax.rem(dev, 2 * n_orb)
+        return rest * blocks + dz * per_dev + k
 
     def transform(p, carry):
         firsts, seconds = [], []
         for s in range(slots):
-            block_m = panel[screen_ref[0, p * slots + s]]
+            block_m = panel[place(screen_ref[0, s, o * own_pairs + p])]
             first = jnp.dot(block_m, ints[p * slots + s], preferred_element_type=F32)
             firsts.append(first.astype(BF))
-            seconds.append(panel[screen_ref[1, p * slots + s]])
+            seconds.append(panel[place(screen_ref[1, s, o * own_pairs + p])])
         halves[p] = lax.dot_general(
             jnp.concatenate(seconds, axis=1),
             jnp.concatenate(firsts, axis=1),
@@ -208,20 +244,29 @@
         )
         return carry
 
-    quarter_pairs = own_pairs // 4
-    lax.fori_loop(0, quarter_pairs, transform, 0)
-
-    for copy in tab_z:
-        copy.wait()
-
-    def tab_view(xx, yy, cc, part):
-        if part is None:
-            return tab_ref.at[cc * 2 + xx, yy]
-        h = pairs // 2
-        return tab_ref.at[cc * 2 + xx, yy, pl.ds(part * h, h)]
-
-    tab_1 = plane_first(tab_view)
-    lax.fori_loop(quarter_pairs, own_pairs, transform, 0)
+    cut = own_pairs // 4
+    lax.fori_loop(0, cut, transform, 0, unroll=2)
+    for k in range(1, nz):
+        tab_z[k - 1].wait()
+        pass_on(k)
+    lax.fori_loop(cut, 2 * cut, transform, 0, unroll=2)
+    second = []
+    for k in range(nz // 2):
+        tab_plane[k][0].wait()
+        part = tab_at(1 - x, y, c, k)
+        second.append(send(part, part, y_peer))
+        tab_plane[k][1].wait()
+    lax.fori_loop(2 * cut, 3 * cut, transform, 0, unroll=2)
+    for k in range(nz // 2, nz):
+        tab_plane[k][1].wait()
+        part = tab_at(x, 1 - y, c, k)
+        second.append(send(part, part, x_peer))
+        tab_plane[k][0].wait()
+    across = [
+        send(tab_at(1 - x, y, c), tab_at(1 - x, y, c), c_peer),
+        send(tab_at(x, 1 - y, c), tab_at(x, 1 - y, c), c_peer),
+    ]
+    lax.fori_loop(3 * cut, own_pairs, transform, 0, unroll=2)
 
     flat = jnp.concatenate([halves[p] for p in range(own_pairs)], axis=1).astype(BF)
     size = own_pairs * i_count
@@ -259,10 +304,15 @@
         return carry
 
     lax.fori_loop(1, n_dev, a2a_start, 0)
-    tab_2 = plane_second(tab_view, tab_1)
-    tab_3 = plane_third(tab_view, tab_1, tab_2)
+    for copy in second:
+        copy.wait()
+    far = tab_at(1 - x, 1 - y, c)
+    across.append(send(far, far, c_peer))
+    for group in tab_plane:
+        group[2].wait()
     lax.fori_loop(1, n_dev, a2a_wait, 0)
-    tab_3.wait()
+    for copy in across:
+        copy.wait()
 
 
 def expand_kernel(per_step, half_ref, tab_ref, out_ref, left_t, right):
@@ -293,16 +343,10 @@
     slots = integrals.shape[1]
     own_pairs = integrals.shape[0] // n_orb
     per_dev = rows // BLK
-    own_screen = lax.dynamic_slice_in_dim(
-        screen, lax.axis_index("orb") * own_pairs, own_pairs, 1
-    ).reshape(2, own_pairs * slots)
-    dev, k = own_screen // per_dev, own_screen % per_dev
-    dz, rest = dev // (2 * n_orb), dev % (2 * n_orb)
-    own_screen = (rest * nz + dz) * per_dev + k
     share = pairs // nz
     j_own = i_count // n_pair
     lanes = own_pairs * i_count // n_orb
-    sends = 2 * (nz - 1) + 8 + 3 + (nz - 1) + 8
+    sends = 3 + 3 * (nz - 1) + 8 + 1 + 4 * nz + 3
     vmem = pl.BlockSpec(memory_space=pltpu.VMEM)
     table, half = pl.pallas_call(
         functools.partial(exchange_kernel, (n_pair, n_orb, nz, own_pairs, slots)),
@@ -312,43 +356,43 @@
         ),
         in_specs=[
             pl.BlockSpec(memory_space=pltpu.SMEM),
-            pl.BlockSpec(memory_space=pl.ANY),
-            vmem,
-            vmem,
+            pl.BlockSpec(memory_space=pltpu.HBM),
+            pl.BlockSpec(memory_space=pltpu.HBM),
+            pl.BlockSpec(memory_space=pltpu.HBM),
             vmem,
         ],
         out_specs=(vmem, vmem),
         scratch_shapes=[
             pltpu.VMEM((own_pairs * slots, BLK, BLK), BF),
             pltpu.VMEM((n_dev * per_dev, i_count, BLK), BF),
-            pltpu.VMEM((2, rows, width // 2), BF),
-            pltpu.VMEM((2, 2, rows, width // 4), BF),
+            pltpu.VMEM((4, rows, width // 4), BF),
             pltpu.VMEM((pairs, width // 4), BF),
             pltpu.VMEM((2, pairs, width // 4), BF),
             pltpu.VMEM((nz - 1, share, width // 4), BF),
             pltpu.VMEM((own_pairs, i_count, i_count), F32),
             pltpu.VMEM((n_dev, j_own, lanes), F32),
             pltpu.SemaphoreType.DMA,
+            pltpu.SemaphoreType.DMA((1 + per_dev,)),
             pltpu.SemaphoreType.DMA((sends,)),
             pltpu.SemaphoreType.DMA((sends,)),
             pltpu.SemaphoreType.DMA((n_dev,)),
             pltpu.SemaphoreType.DMA((n_dev,)),
         ],
         compiler_params=pltpu.CompilerParams(
-            collective_id=0, has_side_effects=True, vmem_limit_bytes=48 * 2**20
+            collective_id=0, has_side_effects=True, vmem_limit_bytes=60 * 2**20
         ),
     )(
-        own_screen,
+        screen.transpose(0, 2, 1),
         integrals.reshape(-1, BLK, BLK),
         occupied.T,
         virtual,
-        pair_index[:, :, None],
+        pair_index,
     )
     k_own = i_count // n_orb
     half = half.reshape(n_dev, j_own, k_own, own_pairs).transpose(1, 2, 0, 3)
     half = half.reshape(j_own * k_own, 1, pairs).astype(BF)
     count = j_own * k_own
-    per_step = 2
+    per_step = 8
     return pl.pallas_call(
         functools.partial(expand_kernel, per_step),
         grid=(count // per_step,),
@@ -356,7 +400,7 @@
         in_specs=[vmem, vmem],
         out_specs=pl.BlockSpec((1, per_step, width, width), lambda s: (0, s, 0, 0)),
         scratch_shapes=[pltpu.VMEM((width, pairs), BF), pltpu.VMEM((pairs, width), BF)],
-        compiler_params=pltpu.CompilerParams(vmem_limit_bytes=48 * 2**20),
+        compiler_params=pltpu.CompilerParams(vmem_limit_bytes=60 * 2**20),
     )(half, table)
 
 
@@ -401,8 +445,7 @@
     n_pair, n_orb = lax.axis_size("pair"), lax.axis_size("orb")
     fits = (
         n_orb == 4
-        and n_pair % 2 == 0
-        and n_pair <= 8
+        and n_pair in (4, 8)
         and args[2].shape[0] % BLK == 0
         and args[4].shape[1] == n_pair * args[0].shape[0]
     )

time: 61.4 us -> 53.3 us (0.87)
  Pallas kernels: 55.8 us -> 51.1 us
  local copies, waits for them, and re-layouts: 3.65 us -> 1.13 us
  other arithmetic: 1.59 us -> 0.85 us
    pallas_call x1, Pallas kernels: 41.4 us -> 38.1 us  [fast_body(): pl.pallas_call(functools.partial(exchange_kernel, (n_pair, n_orb, nz, own...]
    unnamed x4 -> x0, local copies, waits for them, and re-layouts: 1.73 us -> none
    pallas_call x1, Pallas kernels: 14.4 us -> 12.9 us  [fast_body(): pl.pallas_call(functools.partial(expand_kernel, per_step), grid=(count //...]
    broadcast_in_dim x1 -> x0, local copies, waits for them, and re-layouts: 0.9 us -> none  [fast_body(): pair_index[:, :, None]]
    convert_element_type x1, other arithmetic: 0.01 us -> 0.85 us  [fast_body(): half = half.reshape(j_own * k_own, 1, pairs).astype(BF)]
    div x1 -> x0, other arithmetic: 0.78 us -> none  [fast_body(): dev, k = (own_screen // per_dev, own_screen % per_dev)]
    ne x1 -> x0, other arithmetic: 0.77 us -> none  [fast_body(): dev, k = (own_screen // per_dev, own_screen % per_dev)]
    convert_element_type x3, local copies, waits for them, and re-layouts: 0.5 us -> 1.13 us  [fast_body(): half = half.reshape(j_own * k_own, 1, pairs).astype(BF)]
where the time goes in v2:
time: 53.3 us; the launch traced here: 53.1 us
  Pallas kernels  51.1 us (96%)
  local copies, waits for them, and re-layouts  1.13 us (2%)
  other arithmetic  0.85 us (2%)
    pallas_call x1, Pallas kernels, fast_body(): pl.pallas_call(functools.partial(exchange_kernel, (n_pair, n_orb, nz, own...  38.1 us
    pallas_call x1, Pallas kernels, fast_body(): pl.pallas_call(functools.partial(expand_kernel, per_step), grid=(count //...  12.9 us
    convert_element_type x3, local copies, waits for them, and re-layouts, fast_body(): half = half.reshape(j_own * k_own, 1, pairs).astype(BF)  1.13 us

profile of v2, /device:TPU:0, one launch (start us, length us, event | category | flops | bytes accessed | tf_op | source)
XLA Modules:
  0.0 53.1 jit_solution(8436019662159679502)
XLA Ops:
  0.0 38.1 %shard_map.55 = (bf16[4,2,512,128]{3,2,1,0:T(8,128)(2,1)}, f32[32,4,128]{2,1,0:T(4,128)}) custom-call(s32[2,8,64]{2,1,0:T(8,128)} %bitcast.11, bf16[512,128,128]{2,1,0:T(8,128)(2,1)} %bitcast.8, bf16[32,384]{1,0:T(8,128)(2,1)} %bitcast.10, bf16[384,512]{1,0:T(8,128)(2,1)} %vir_ref.1, s32[2,512]{1,0:T(2,128)} %pidx_ref.1), custom_call_target="tpu_custom_call" | custom-call | tf_op jit(solution)/shard_map/pallas_call | solution.py:351
  38.1 0.9 %convert_element_type.9 = bf16[32,4,128]{2,1,0:T(4,128)(2,1)S(1)} convert(f32[32,4,128]{2,1,0:T(4,128)} %get-tuple-element.7) | non-fusion elementwise | flops 16384 | bytes 98304 | tf_op jit(solution)/shard_map/convert_element_type | solution.py:393
  39.0 0.1 copy.7
  39.1 0.2 copy.8
  39.3 0.8 %convert_element_type.13.half_ref = bf16[32,1,512]{2,1,0:T(2,128)(2,1)} reshape(bf16[4,8,32,16]{3,2,1,0:T(8,128)(2,1)S(1)} %copy.8) | data formatting | bytes 65536 | tf_op jit(solution)/shard_map/convert_element_type | solution.py:393
  40.1 12.9 %shard_map.56 = bf16[1,32,512,512]{3,2,1,0:T(8,128)(2,1)} custom-call(bf16[32,1,512]{2,1,0:T(2,128)(2,1)} %convert_element_type.13.half_ref, bf16[4,2,512,128]{3,2,1,0:T(8,128)(2,1)} %get-tuple-element.8.tab_ref), custom_call_target="tpu_custom_call" | custom-call | tf_op jit(solution)/shard_map/pallas_call | solution.py:396

commit v3 on v2

--- a/solution.py
+++ b/solution.py
@@ -197,30 +197,6 @@
             )
         )
     occ_3 = plane_third(occ_view, occ_1, occ_2)
-    for copy in vir_z:
-        copy.wait()
-    def rows_of(k):
-        zz = lax.rem(z - k + nz, nz)
-        return pl.ds(pl.multiple_of(zz * share, share), share)
-
-    def tab_at(xx, yy, cc, k=None):
-        if k is None:
-            return tab_ref.at[xx * 2 + yy, cc]
-        return tab_ref.at[xx * 2 + yy, cc, rows_of(k)]
-
-    total = mine[1, rows_of(0)]
-    for k in range(nz - 1):
-        total = total + from_z[k]
-    tab_ref[x * 2 + y, c, rows_of(0)] = total
-    tab_z = z_spread(tab_at(x, y, c, 0))
-    tab_plane = []
-
-    def pass_on(k):
-        part = tab_at(x, y, c, k)
-        tab_plane.append([send(part, part, p) for p in (x_peer, y_peer, c_peer)])
-
-    pass_on(0)
-
     fetch.wait()
     occ_3.wait()
 
@@ -246,17 +222,41 @@
 
     cut = own_pairs // 4
     lax.fori_loop(0, cut, transform, 0, unroll=2)
+    for copy in vir_z:
+        copy.wait()
+    def rows_of(k):
+        zz = lax.rem(z - k + nz, nz)
+        return pl.ds(pl.multiple_of(zz * share, share), share)
+
+    def tab_at(xx, yy, cc, k=None):
+        if k is None:
+            return tab_ref.at[xx * 2 + yy, cc]
+        return tab_ref.at[xx * 2 + yy, cc, rows_of(k)]
+
+    total = mine[1, rows_of(0)]
+    for k in range(nz - 1):
+        total = total + from_z[k]
+    tab_ref[x * 2 + y, c, rows_of(0)] = total
+    tab_z = z_spread(tab_at(x, y, c, 0))
+    tab_plane = []
+
+    def pass_on(k):
+        part = tab_at(x, y, c, k)
+        tab_plane.append([send(part, part, p) for p in (x_peer, y_peer, c_peer)])
+
+    pass_on(0)
+
+    lax.fori_loop(cut, 3 * cut, transform, 0, unroll=2)
     for k in range(1, nz):
         tab_z[k - 1].wait()
         pass_on(k)
-    lax.fori_loop(cut, 2 * cut, transform, 0, unroll=2)
+    lax.fori_loop(3 * cut, own_pairs, transform, 0, unroll=2)
     second = []
     for k in range(nz // 2):
         tab_plane[k][0].wait()
         part = tab_at(1 - x, y, c, k)
         second.append(send(part, part, y_peer))
         tab_plane[k][1].wait()
-    lax.fori_loop(2 * cut, 3 * cut, transform, 0, unroll=2)
     for k in range(nz // 2, nz):
         tab_plane[k][1].wait()
         part = tab_at(x, 1 - y, c, k)
@@ -266,7 +266,6 @@
         send(tab_at(1 - x, y, c), tab_at(1 - x, y, c), c_peer),
         send(tab_at(x, 1 - y, c), tab_at(x, 1 - y, c), c_peer),
     ]
-    lax.fori_loop(3 * cut, own_pairs, transform, 0, unroll=2)
 
     flat = jnp.concatenate([halves[p] for p in range(own_pairs)], axis=1).astype(BF)
     size = own_pairs * i_count
@@ -400,7 +399,7 @@
         in_specs=[vmem, vmem],
         out_specs=pl.BlockSpec((1, per_step, width, width), lambda s: (0, s, 0, 0)),
         scratch_shapes=[pltpu.VMEM((width, pairs), BF), pltpu.VMEM((pairs, width), BF)],
-        compiler_params=pltpu.CompilerParams(vmem_limit_bytes=60 * 2**20),
+        compiler_params=pltpu.CompilerParams(vmem_limit_bytes=32 * 2**20),
     )(half, table)
 
 

time: 53.3 us -> 52 us (0.976)
  Pallas kernels: 51.1 us -> 49.1 us
  local copies, waits for them, and re-layouts: 1.13 us -> 1.71 us
    pallas_call x1, Pallas kernels: 12.9 us -> 11.6 us  [fast_body(): pl.pallas_call(functools.partial(expand_kernel, per_step), grid=(count //...]
    unnamed x0 -> x2, local copies, waits for them, and re-layouts: none -> 1.22 us
    pallas_call x1, Pallas kernels: 38.1 us -> 37.5 us  [fast_body(): pl.pallas_call(functools.partial(exchange_kernel, (n_pair, n_orb, nz, own...]
    convert_element_type x3, local copies, waits for them, and re-layouts: 1.13 us -> 0.5 us  [fast_body(): half = half.reshape(j_own * k_own, 1, pairs).astype(BF)]
where the time goes in v3:
time: 52 us; the launch traced here: 51.7 us
  Pallas kernels  49.1 us (94%)
  local copies, waits for them, and re-layouts  1.71 us (3%)
  other arithmetic  0.85 us (2%)
    pallas_call x1, Pallas kernels, fast_body(): pl.pallas_call(functools.partial(exchange_kernel, (n_pair, n_orb, nz, own...  37.5 us
    pallas_call x1, Pallas kernels, fast_body(): pl.pallas_call(functools.partial(expand_kernel, per_step), grid=(count //...  11.6 us
    unnamed x2, local copies, waits for them, and re-layouts  1.22 us

profile of v3, /device:TPU:0, one launch (start us, length us, event | category | flops | bytes accessed | tf_op | source)
XLA Modules:
  0.0 51.7 jit_solution(17219963330268698345)
XLA Ops:
  0.0 37.5 %shard_map.55 = (bf16[4,2,512,128]{3,2,1,0:T(8,128)(2,1)}, f32[32,4,128]{2,1,0:T(4,128)}) custom-call(s32[2,8,64]{2,1,0:T(8,128)} %bitcast.11, bf16[512,128,128]{2,1,0:T(8,128)(2,1)} %bitcast.8, bf16[32,384]{1,0:T(8,128)(2,1)} %bitcast.10, bf16[384,512]{1,0:T(8,128)(2,1)} %vir_ref.1, s32[2,512]{1,0:T(2,128)} %pidx_ref.1), custom_call_target="tpu_custom_call" | custom-call | tf_op jit(solution)/shard_map/pallas_call | solution.py:350
  37.5 0.9 %convert_element_type.9 = bf16[32,4,128]{2,1,0:T(4,128)(2,1)S(1)} convert(f32[32,4,128]{2,1,0:T(4,128)} %get-tuple-element.7) | non-fusion elementwise | flops 16384 | bytes 98304 | tf_op jit(solution)/shard_map/convert_element_type | solution.py:392
  38.3 0.1 copy.7
  38.5 0.2 copy.8
  38.7 0.2 convert_element_type.13.half_ref
  38.8 0.0 copy-start
  38.9 1.2 %copy-done = bf16[4,2,512,128]{3,2,1,0:T(8,128)(2,1)S(1)} copy-done((bf16[4,2,512,128]{3,2,1,0:T(8,128)(2,1)S(1)}, bf16[4,2,512,128]{3,2,1,0:T(8,128)(2,1)}, u32[]{:S(2)}) %copy-start) | copy-done | bytes 1048600
  40.1 11.6 %shard_map.56 = bf16[1,32,512,512]{3,2,1,0:T(8,128)(2,1)} custom-call(bf16[32,1,512]{2,1,0:T(2,128)(2,1)S(1)} %convert_element_type.13.half_ref, bf16[4,2,512,128]{3,2,1,0:T(8,128)(2,1)S(1)} %copy-done), custom_call_target="tpu_custom_call" | custom-call | tf_op jit(solution)/shard_map/pallas_call | solution.py:395
Async XLA Ops:
  38.8 1.2 %copy-start = (bf16[4,2,512,128]{3,2,1,0:T(8,128)(2,1)S(1)}, bf16[4,2,512,128]{3,2,1,0:T(8,128)(2,1)}, u32[]{:S(2)}) copy-start(bf16[4,2,512,128]{3,2,1,0:T(8,128)(2,1)} %get-tuple-element.8.tab_ref) | copy-start | bytes 3145732
